TPU v7x, 32 devices: a whole 2x2x4 slice. The times are simulated.
32 devices in a mesh: ctx: 16 (over z, y, core), head: 2 (over x).
Axes of the slice: x: 2, y: 2, z: 4, core: 2. Of those that a mesh axis runs over, the one named last changes fastest.
Arguments:
- queries: bfloat16 [32768, 2048], P('ctx', 'head'), may hold values from -6 to 6
- key_vectors: bfloat16 [32768, 2048], P('ctx', 'head'), may hold values from -6 to 6
- values: bfloat16 [32768, 2048], P('ctx', 'head'), may hold values from -6 to 6
- out_grad: bfloat16 [32768, 2048], P('ctx', 'head'), may hold values from -6 to 6
- level_logits: float32 [16, 5, 32768], P('head', None, 'ctx'), may hold values from -6 to 6
- level_proj: bfloat16 [80, 2048], P(None, 'head'), may hold values from -0.3125 to 0.3125
Outputs:
- grad_queries: bfloat16 [32768, 2048], P('ctx', 'head')
- grad_keys: bfloat16 [32768, 2048], P('ctx', 'head')
- grad_values: bfloat16 [32768, 2048], P('ctx', 'head')
- level_grad: float32 [16, 5, 32768], P('head', None, 'ctx')
- hidden_grad: bfloat16 [32768, 2048], P('ctx', 'head')
All inputs are finite; a program needn't handle non-finite values.
Results may differ from a plain program's by a relative error of at most 0.0058.
Values may be sent and summed in bfloat16 or wider, within the bound.
A program may use at most 384 MiB of HBM per device.

v0:
```python
import jax
import jax.numpy as jnp
from jax import lax
from jax.sharding import PartitionSpec as P

HIGHEST = lax.Precision.HIGHEST


def partner(shard, axis, distance):
    return lax.ppermute(shard, axis, [(i, i ^ 1 << distance) for i in range(lax.axis_size(axis))])


def group_terms(query_heads, key_heads, value_heads, cotan_heads, gate_zero, scaling):
    row_count = query_heads.shape[0]
    blk_rows = min(1024, row_count)
    positions = jnp.arange(row_count, dtype=jnp.int32)

    def one_block(totals, blk_index):
        grad_keys, grad_values = totals
        blk_start = blk_index * blk_rows
        query_blk = lax.dynamic_slice_in_dim(query_heads, blk_start, blk_rows, 0)
        cotan_blk = lax.dynamic_slice_in_dim(cotan_heads, blk_start, blk_rows, 0)
        gate_blk = lax.dynamic_slice_in_dim(gate_zero, blk_start, blk_rows, 1)
        causal = positions[None, :] <= (blk_start + jnp.arange(blk_rows, dtype=jnp.int32))[:, None]
        weight = jnp.where(causal[None], scaling * gate_blk[:, :, None], 0.0)
        scores = jnp.einsum(
            "qhd,khd->hqk", query_blk, key_heads, preferred_element_type=jnp.float32
        )
        products = jnp.einsum(
            "qhd,khd->hqk", cotan_blk, value_heads, preferred_element_type=jnp.float32
        )
        prod_weighted = (weight * products).astype(jnp.bfloat16)
        score_weighted = (weight * scores).astype(jnp.bfloat16)
        gate_grad = scaling * jnp.sum(jnp.where(causal[None], scores * products, 0.0), axis=2)
        query_grad = jnp.einsum(
            "hqk,khd->qhd", prod_weighted, key_heads, preferred_element_type=jnp.float32
        )
        grad_keys = grad_keys + jnp.einsum(
            "hqk,qhd->khd", prod_weighted, query_blk, preferred_element_type=jnp.float32
        )
        grad_values = grad_values + jnp.einsum(
            "hqk,qhd->khd", score_weighted, cotan_blk, preferred_element_type=jnp.float32
        )
        return ((grad_keys, grad_values), (query_grad, gate_grad))

    zero_grads = jnp.zeros(key_heads.shape, jnp.float32)
    block_ids = jnp.arange(row_count // blk_rows, dtype=jnp.int32)
    (grad_keys, grad_values), (query_grads, gate_grads) = lax.scan(
        one_block, (zero_grads, zero_grads), block_ids
    )
    query_grad = query_grads.reshape(key_heads.shape)
    gate_grad = jnp.transpose(gate_grads, (1, 0, 2)).reshape(gate_zero.shape)
    return (query_grad, grad_keys, grad_values, gate_grad)


def body(queries, key_vectors, values, out_grad, level_logits, level_proj):
    row_count = queries.shape[0]
    head_count = level_logits.shape[0]
    head_size = queries.shape[1] // head_count
    scaling = float(head_size * row_count * lax.axis_size("ctx")) ** (-0.5)
    query_heads = queries.reshape(row_count, head_count, head_size)
    key_heads = key_vectors.reshape(row_count, head_count, head_size)
    value_heads = values.reshape(row_count, head_count, head_size)
    cotan_heads = out_grad.reshape(row_count, head_count, head_size)
    gates = jax.nn.softplus(level_logits)
    local_q, local_k, local_v, gate_zero_grad = group_terms(
        query_heads, key_heads, value_heads, cotan_heads, gates[:, 0], scaling
    )
    kv_state = jnp.einsum(
        "chd,che->hde", key_heads, value_heads, preferred_element_type=jnp.float32
    )
    bit_count = lax.axis_size("ctx").bit_length() - 1
    own_index = lax.axis_index("ctx")
    add_incoming = lax.all_gather(kv_state[None], "ctx", axis=0, tiled=True)
    device_ids = jnp.arange(add_incoming.shape[0], dtype=jnp.int32)
    shifts = jnp.arange(bit_count, dtype=jnp.int32)[:, None]
    own_prefix = jnp.right_shift(own_index, shifts)
    inside = (jnp.right_shift(device_ids[None, :], shifts) == jnp.bitwise_xor(own_prefix, 1)) & (
        jnp.bitwise_and(own_prefix, 1) == 1
    )
    collected = jnp.einsum(
        "bn,nhde->bhde", inside.astype(jnp.float32), add_incoming, precision=HIGHEST
    )
    level_states = [collected[bit_pos] for bit_pos in range(bit_count)]
    grad_q = local_q
    level_terms = [gate_zero_grad]
    adjoints = []
    for bit_pos in range(bit_count):
        is_upper = jnp.bitwise_and(jnp.right_shift(own_index, bit_pos), 1).astype(jnp.float32)
        weights = scaling * gates[:, bit_pos + 1]
        state_bf = level_states[bit_pos].astype(jnp.bfloat16)
        mapped = jnp.einsum(
            "che,hde->chd", cotan_heads, state_bf, preferred_element_type=jnp.float32
        )
        grad_q = grad_q + weights.T[:, :, None] * mapped
        reached = jnp.einsum(
            "chd,hde->che", query_heads, state_bf, preferred_element_type=jnp.float32
        )
        level_terms.append(scaling * jnp.sum(reached * cotan_heads, axis=2).T)
        weighted = (weights.T[:, :, None] * query_heads).astype(jnp.bfloat16)
        adjoint = jnp.einsum(
            "chd,che->hde", weighted, cotan_heads, preferred_element_type=jnp.float32
        )
        adjoints.append(is_upper * adjoint)
    carried = jnp.zeros_like(kv_state)
    for bit_pos in range(bit_count):
        is_lower = 1.0 - jnp.bitwise_and(jnp.right_shift(own_index, bit_pos), 1).astype(jnp.float32)
        sending = jnp.stack(adjoints[bit_pos:], axis=0)
        incoming = partner(sending, "ctx", bit_pos)
        carried = carried + is_lower * incoming[0]
        for later in range(bit_pos + 1, bit_count):
            adjoints[later] = adjoints[later] + incoming[later - bit_pos]
    carried_bf = carried.astype(jnp.bfloat16)
    grad_k = local_k + jnp.einsum(
        "che,hde->chd", value_heads, carried_bf, preferred_element_type=jnp.float32
    )
    grad_v = local_v + jnp.einsum(
        "chd,hde->che", key_heads, carried_bf, preferred_element_type=jnp.float32
    )
    level_grad = jnp.stack(level_terms, axis=1) * jax.nn.sigmoid(level_logits)
    logit_cot = level_grad.astype(jnp.bfloat16).reshape(-1, row_count)
    hidden_grad = lax.dot_general(
        lax.all_gather(logit_cot, "head", axis=0, tiled=True),
        level_proj,
        (((0,), (0,)), ((), ())),
        preferred_element_type=jnp.float32,
    )
    return (
        grad_q.reshape(row_count, -1).astype(jnp.bfloat16),
        grad_k.reshape(row_count, -1).astype(jnp.bfloat16),
        grad_v.reshape(row_count, -1).astype(jnp.bfloat16),
        level_grad,
        hidden_grad.astype(jnp.bfloat16),
    )


def solution(mesh):
    in_specs = (
        P("ctx", "head"),
        P("ctx", "head"),
        P("ctx", "head"),
        P("ctx", "head"),
        P("head", None, "ctx"),
        P(None, "head"),
    )
    out_specs = (
        P("ctx", "head"),
        P("ctx", "head"),
        P("ctx", "head"),
        P("head", None, "ctx"),
        P("ctx", "head"),
    )
    return jax.shard_map(body, mesh=mesh, in_specs=in_specs, out_specs=out_specs, check_vma=False)
```

profile of v0, /device:TPU:0, one launch (start us, length us, event | category | flops | bytes accessed | tf_op | source)
XLA Modules:
  0.0 722.1 jit_solution(1613798597561512942)
XLA Ops:
  8.5 6.5 copy.110
  15.0 6.4 copy.111
  21.4 4.9 fusion.77
  31.9 3.8 collective-permute-done
  36.0 3.0 collective-permute-start.1
  39.0 34.7 %collective-permute-done.1 = f32[3,8,128,128]{3,2,1,0:T(8,128)S(1)} collective-permute-done((f32[3,8,128,128]{3,2,1,0:T(8,128)S(1)}, f32[3,8,128,128]{3,2,1,0:T(8,128)S(1)}, u32[]{:S(2)}, u32[]{:S(2)}) %collective-permute-start.1) | collective-permute-done | bytes 1572896 | tf_op jit(solution)/shard_map/ppermute | solution.py:10
  75.9 1.8 collective-permute-start.2
  77.7 6.5 copy.113
  84.2 6.4 copy.112
  90.6 5.5 fusion.129
  96.2 6.5 copy.116
  102.7 6.5 copy.115
  109.2 2.1 fusion.81
  111.3 2.6 collective-permute-start.3
  113.9 493.6 %while.17 = (s32[]{:T(128)}, f32[2048,8,128]{0,2,1:T(8,128)}, f32[2048,8,128]{0,2,1:T(8,128)}, f32[2,1024,8,128]{1,0,3,2:T(2,128)}, f32[2,8,1024]{2,1,0:T(8,128)...) while((s32[]{:T(128)}, f32[2048,8,128]{0,2,1:T(8,128)}, ...), condition=%wide.region_2.3_spmd.clone, body=%wide.region_0.2_spmd.clone.sunk | while | flops 21686657024 | bytes 488906976 | solution.py:48
  125.2 1.7 iota_compare_fusion.2
  126.9 26.8 %fusion.172 = f32[8,1024,2048]{2,1,0:T(8,128)} fusion(bf16[2048,8,128]{2,0,1:T(8,128)(2,1)} %get-tuple-element.326, bf16[2048,8,128]{0,2,1:T(8,128)(2,1)} %get-tuple-element.325, s32[]{:T(128)S(6)} %select_n.48), kind=kOutput, calls=%fused_computation.16.clone.1 | convolution fusion | flops 4294967296 | bytes 73400320 | tf_op jit(solution)/shard_map/while/body/eval_jaxpr/qhd,khd->hqk/dot_general | solution.py:29
  153.8 27.1 %fusion.173 = f32[1,1024,8,128]{3,1,2,0:T(8,128)} fusion(bf16[2048,8,128]{2,0,1:T(8,128)(2,1)} %get-tuple-element.327, f32[8,1024,2048]{2,1,0:T(8,128)} %fusion.172, f32[8,1024]{1,0:T(8,128)S(1)} %dynamic-slice_multiply_fusion.2, pred[1024,2048]{1,0:T(8,128)(4,1)S(1)} %iota_compare_fusion.2), kind=kOutput, calls=%fused_computation.15.clone.1 | convolution fusion | flops 4345298944 | bytes 77627392 | tf_op jit(solution)/shard_map/while/body/eval_jaxpr/hqk,khd->qhd/dot_general | solution.py:35
  180.8 11.1 %copy.214 = f32[1,1024,8,128]{1,0,3,2:T(1,128)} copy(f32[1,1024,8,128]{3,1,2,0:T(8,128)} %fusion.173) | data formatting | bytes 8388608 | tf_op jit(solution)/shard_map/while/body/jit(dynamic_update_index_in_dim)/dynamic_update_slice | solution.py:48
  192.0 71.7 %dynamic_update_slice.14 = f32[2,1024,8,128]{1,0,3,2:T(2,128)} dynamic-update-slice(f32[2,1024,8,128]{1,0,3,2:T(2,128)} %get-tuple-element.305, f32[1,1024,8,128]{1,0,3,2:T(1,128)} %copy.214, s32[]{:T(128)S(6)} %copy.222, s32[]{:T(128)} %constant.23.clone.1..sunk, s32[]{:T(128)} %constant.23.clone.1..sunk, s32[]{:T(128)} %constant.23.clone.1..sunk) | dynamic-update-slice | bytes 8388612 | tf_op jit(solution)/shard_map/while/body/jit(dynamic_update_index_in_dim)/dynamic_update_slice | solution.py:48
  263.7 27.5 %bitcast_add_fusion.6 = f32[2048,8,128]{0,2,1:T(8,128)} fusion(f32[2048,8,128]{0,2,1:T(8,128)} %get-tuple-element.303, pred[]{:T(512)S(6)} %compare.3, f32[8,1024,2048]{2,1,0:T(8,128)} %fusion.172, f32[8,1024]{1,0:T(8,128)S(1)} %dynamic-slice_multiply_fusion.2, pred[1024,2048]{1,0:T(8,128)(4,1)S(1)} %iota_compare_fusion.2, ...), kind=kOutput, calls=%fused_computation.11.clone.1 | convolution fusion | flops 4349493248 | bytes 88113160 | tf_op jit(solution)/shard_map/while/body/eval_jaxpr/hqk,qhd->khd/dot_general | solution.py:38
  291.2 45.4 %select_reduce_fusion.2 = (f32[8,1024]{1,0:T(8,128)S(1)}, f32[8,1024,2048]{2,1,0:T(8,128)}) fusion(f32[8,1024,2048]{2,1,0:T(8,128)} %fusion.172, pred[1024,2048]{1,0:T(8,128)(4,1)S(1)} %iota_compare_fusion.2, bf16[2048,8,128]{2,0,1:T(8,128)(2,1)} %get-tuple-element.327, bf16[2048,8,128]{0,2,1:T(8,128)(2,1)} %get-tuple-element.323, s32[]{:T(128)S(6)} %select_n.48), kind=kOutput, calls=%fused_computation.5.clone.2 | convolution fusion | flops 4345290752 | bytes 142639104 | tf_op jit(solution)/shard_map/while/body/eval_jaxpr/qhd,khd->hqk/dot_general | solution.py:26
  336.6 27.5 %bitcast_add_fusion.7 = f32[2048,8,128]{0,2,1:T(8,128)} fusion(f32[2048,8,128]{0,2,1:T(8,128)} %get-tuple-element.304, f32[8,1024,2048]{2,1,0:T(8,128)} %get-tuple-element.285, f32[8,1024]{1,0:T(8,128)S(1)} %dynamic-slice_multiply_fusion.2, pred[1024,2048]{1,0:T(8,128)(4,1)S(1)} %iota_compare_fusion.2, pred[]{:T(512)S(6)} %compare.3, ...), kind=kOutput, calls=%fused_computation.10.clone.1 | convolution fusion | flops 4349493248 | bytes 88113160 | tf_op jit(solution)/shard_map/while/body/eval_jaxpr/hqk,qhd->khd/dot_general | solution.py:41
  365.3 1.7 iota_compare_fusion.2
  367.0 25.7 %fusion.172 = f32[8,1024,2048]{2,1,0:T(8,128)} fusion(bf16[2048,8,128]{2,0,1:T(8,128)(2,1)} %get-tuple-element.326, bf16[2048,8,128]{0,2,1:T(8,128)(2,1)} %get-tuple-element.325, s32[]{:T(128)S(6)} %select_n.48), kind=kOutput, calls=%fused_computation.16.clone.1 | convolution fusion | flops 4294967296 | bytes 73400320 | tf_op jit(solution)/shard_map/while/body/eval_jaxpr/qhd,khd->hqk/dot_general | solution.py:29
  392.8 26.4 %fusion.173 = f32[1,1024,8,128]{3,1,2,0:T(8,128)} fusion(bf16[2048,8,128]{2,0,1:T(8,128)(2,1)} %get-tuple-element.327, f32[8,1024,2048]{2,1,0:T(8,128)} %fusion.172, f32[8,1024]{1,0:T(8,128)S(1)} %dynamic-slice_multiply_fusion.2, pred[1024,2048]{1,0:T(8,128)(4,1)S(1)} %iota_compare_fusion.2), kind=kOutput, calls=%fused_computation.15.clone.1 | convolution fusion | flops 4345298944 | bytes 77627392 | tf_op jit(solution)/shard_map/while/body/eval_jaxpr/hqk,khd->qhd/dot_general | solution.py:35
  419.2 11.0 %copy.214 = f32[1,1024,8,128]{1,0,3,2:T(1,128)} copy(f32[1,1024,8,128]{3,1,2,0:T(8,128)} %fusion.173) | data formatting | bytes 8388608 | tf_op jit(solution)/shard_map/while/body/jit(dynamic_update_index_in_dim)/dynamic_update_slice | solution.py:48
  430.2 71.7 %dynamic_update_slice.14 = f32[2,1024,8,128]{1,0,3,2:T(2,128)} dynamic-update-slice(f32[2,1024,8,128]{1,0,3,2:T(2,128)} %get-tuple-element.305, f32[1,1024,8,128]{1,0,3,2:T(1,128)} %copy.214, s32[]{:T(128)S(6)} %copy.222, s32[]{:T(128)} %constant.23.clone.1..sunk, s32[]{:T(128)} %constant.23.clone.1..sunk, s32[]{:T(128)} %constant.23.clone.1..sunk) | dynamic-update-slice | bytes 8388612 | tf_op jit(solution)/shard_map/while/body/jit(dynamic_update_index_in_dim)/dynamic_update_slice | solution.py:48
  501.9 29.9 %bitcast_add_fusion.6 = f32[2048,8,128]{0,2,1:T(8,128)} fusion(f32[2048,8,128]{0,2,1:T(8,128)} %get-tuple-element.303, pred[]{:T(512)S(6)} %compare.3, f32[8,1024,2048]{2,1,0:T(8,128)} %fusion.172, f32[8,1024]{1,0:T(8,128)S(1)} %dynamic-slice_multiply_fusion.2, pred[1024,2048]{1,0:T(8,128)(4,1)S(1)} %iota_compare_fusion.2, ...), kind=kOutput, calls=%fused_computation.11.clone.1 | convolution fusion | flops 4349493248 | bytes 88113160 | tf_op jit(solution)/shard_map/while/body/eval_jaxpr/hqk,qhd->khd/dot_general | solution.py:38
  531.8 45.4 %select_reduce_fusion.2 = (f32[8,1024]{1,0:T(8,128)S(1)}, f32[8,1024,2048]{2,1,0:T(8,128)}) fusion(f32[8,1024,2048]{2,1,0:T(8,128)} %fusion.172, pred[1024,2048]{1,0:T(8,128)(4,1)S(1)} %iota_compare_fusion.2, bf16[2048,8,128]{2,0,1:T(8,128)(2,1)} %get-tuple-element.327, bf16[2048,8,128]{0,2,1:T(8,128)(2,1)} %get-tuple-element.323, s32[]{:T(128)S(6)} %select_n.48), kind=kOutput, calls=%fused_computation.5.clone.2 | convolution fusion | flops 4345290752 | bytes 142639104 | tf_op jit(solution)/shard_map/while/body/eval_jaxpr/qhd,khd->hqk/dot_general | solution.py:26
  577.2 29.9 %bitcast_add_fusion.7 = f32[2048,8,128]{0,2,1:T(8,128)} fusion(f32[2048,8,128]{0,2,1:T(8,128)} %get-tuple-element.304, f32[8,1024,2048]{2,1,0:T(8,128)} %get-tuple-element.285, f32[8,1024]{1,0:T(8,128)S(1)} %dynamic-slice_multiply_fusion.2, pred[1024,2048]{1,0:T(8,128)(4,1)S(1)} %iota_compare_fusion.2, pred[]{:T(512)S(6)} %compare.3, ...), kind=kOutput, calls=%fused_computation.10.clone.1 | convolution fusion | flops 4349493248 | bytes 88113160 | tf_op jit(solution)/shard_map/while/body/eval_jaxpr/hqk,qhd->khd/dot_general | solution.py:41
  607.5 11.8 %reshape.123 = f32[2048,8,128]{0,2,1:T(8,128)} reshape(f32[2,1024,8,128]{1,0,3,2:T(2,128)} %get-tuple-element.70) | data formatting | bytes 16777216 | tf_op jit(solution)/shard_map/reshape | solution.py:51
  619.3 1.7 fusion.84
  621.0 7.9 %fusion.41 = bf16[2048,8,128]{0,2,1:T(8,128)(2,1)} fusion(f32[2048,8,128]{0,2,1:T(8,128)} %get-tuple-element.72, bf16[2048,8,128]{0,2,1:T(8,128)(2,1)} %bitcast.244, bf16[1,8,128,128]{3,2,1,0:T(8,128)(2,1)S(1)} %fusion.84), kind=kOutput, calls=%fused_computation.49 | convolution fusion | flops 541065216 | bytes 17039360 | tf_op jit(solution)/shard_map/chd,hde->che/dot_general | solution.py:117
  629.0 6.4 copy.142
  635.3 7.9 %fusion.42 = bf16[2048,8,128]{0,2,1:T(8,128)(2,1)} fusion(f32[2048,8,128]{0,2,1:T(8,128)} %get-tuple-element.71, bf16[2048,8,128]{0,2,1:T(8,128)(2,1)} %bitcast.241, bf16[1,8,128,128]{3,2,1,0:T(8,128)(2,1)S(1)} %fusion.84), kind=kOutput, calls=%fused_computation.51 | convolution fusion | flops 541065216 | bytes 17039360 | tf_op jit(solution)/shard_map/che,hde->chd/dot_general | solution.py:114
  643.2 6.4 copy.141
  649.6 11.1 %fusion.62 = bf16[4,8,128,128]{3,0,2,1:T(4,128)(2,1)S(1)} fusion(f32[16,8,128,128]{3,2,1,0:T(8,128)} %bitcast.248, s32[4]{0:T(128)S(1)} %fusion.125, pred[4]{0:T(512)(128)(4,1)S(1)} %and_compare_fusion), kind=kOutput, calls=%fused_computation.74 | convolution fusion | flops 101187776 | bytes 9437204 | tf_op jit(solution)/shard_map/bn,nhde->bhde/dot_general | solution.py:81
  660.7 1.8 fusion.128
  664.3 4.5 fusion.102
  668.8 1.5 fusion.39
  670.3 4.5 fusion.96
  676.3 4.5 fusion.99
  680.7 1.5 fusion.40
  683.3 6.0 all_gather.7
  689.3 16.0 %fusion.44 = bf16[2048,8,128]{0,2,1:T(8,128)(2,1)} fusion(f32[8,128,2048]{2,1,0:T(8,128)} %fusion.96, f32[8,128,2048]{2,1,0:T(8,128)} %fusion.99, f32[2048,8,128]{0,2,1:T(8,128)} %reshape.123, f32[8,128,2048]{2,1,0:T(8,128)} %fusion.102, bf16[2048,8,128]{0,2,1:T(8,128)(2,1)} %get-tuple-element.333, f32[2048,8]{0,1:T(8,128)S(1)} %copy-done.11, ...), kind=kOutput, calls=%fused_computation.54 | convolution fusion | flops 555745280 | bytes 42467328 | tf_op jit(solution)/shard_map/che,hde->chd/dot_general | solution.py:92
  705.3 6.4 copy.140
  711.7 3.3 convolution_convert_fusion
  (73 shorter events, 15.0 us)
Async XLA Ops:
  7.2 704.5 %copy-start = (bf16[80,1024]{1,0:T(8,128)(2,1)S(1)}, bf16[80,1024]{1,0:T(8,128)(2,1)}, u32[]{:S(2)}) copy-start(bf16[80,1024]{1,0:T(8,128)(2,1)} %param.13) | copy-start | bytes 491524
  7.2 642.4 %all-gather.3.cloned.1.call-start = ((), (), s32[]{:S(2)}) async-start(), calls=%async_computation | async-start | bytes 8912896 | tf_op jit(solution)/shard_map/all_gather | solution.py:74
  8.5 13.0 %copy-start.10 = (f32[2048,8]{0,1:T(8,128)}, f32[2048,8]{0,1:T(8,128)S(1)}, u32[]{:S(2)}) copy-start(f32[2048,8]{0,1:T(8,128)S(1)} %get-tuple-element.212) | copy-start | bytes 196612
  8.5 17.8 %copy-start.12 = (f32[2048,8]{0,1:T(8,128)}, f32[2048,8]{0,1:T(8,128)S(1)}, u32[]{:S(2)}) copy-start(f32[2048,8]{0,1:T(8,128)S(1)} %get-tuple-element.213) | copy-start | bytes 196612
  8.5 20.1 %copy-start.14 = (f32[2048,8]{0,1:T(8,128)}, f32[2048,8]{0,1:T(8,128)S(1)}, u32[]{:S(2)}) copy-start(f32[2048,8]{0,1:T(8,128)S(1)} %get-tuple-element.214) | copy-start | bytes 196612
  8.5 21.4 %copy-start.8 = (f32[2048,8]{0,1:T(8,128)}, f32[2048,8]{0,1:T(8,128)S(1)}, u32[]{:S(2)}) copy-start(f32[2048,8]{0,1:T(8,128)S(1)} %get-tuple-element.211) | copy-start | bytes 196612
  21.4 4.9 copy-start.1
  21.4 5.9 copy-start.3
  31.4 4.3 collective-permute-start
  35.7 73.5 %copy-start.5 = (f32[4,8,128,128]{3,2,1,0:T(8,128)}, f32[4,8,128,128]{3,2,1,0:T(8,128)S(1)}, u32[]{:S(2)}) copy-start(f32[4,8,128,128]{3,2,1,0:T(8,128)S(1)} %collective-permute-done) | copy-start | bytes 6291460
  36.0 37.7 %collective-permute-start.1 = (f32[3,8,128,128]{3,2,1,0:T(8,128)S(1)}, f32[3,8,128,128]{3,2,1,0:T(8,128)S(1)}, u32[]{:S(2)}, u32[]{:S(2)}) collective-permute-start(f32[3,8,128,128]{3,2,1,0:T(8,128)S(1)} %pad_maximum_fusion.1), channel_id=1, source_target_pairs={{0,4},{2,6},{4,0},{6,2},{8,12},{10,14},{12,8},{14,10},{16,20},{18,... | collective-permute-start | bytes 4718600 | tf_op jit(solution)/shard_map/ppermute | solution.py:10
  73.7 1.1 copy-start.6
  75.9 33.3 %collective-permute-start.2 = (f32[2,8,128,128]{3,2,1,0:T(8,128)}, f32[2,8,128,128]{3,2,1,0:T(8,128)}, u32[]{:S(2)}, u32[]{:S(2)}) collective-permute-start(f32[2,8,128,128]{3,2,1,0:T(8,128)} %pad_maximum_fusion.2), channel_id=1, source_target_pairs={{0,8},{2,10},{4,12},{6,14},{8,0},{10,2},{12,4},{14,6},{16,24},{18,... | collective-permute-start | bytes 3145736 | tf_op jit(solution)/shard_map/ppermute | solution.py:10
  111.3 508.1 %collective-permute-start.3 = (f32[1,8,128,128]{3,2,1,0:T(8,128)}, f32[1,8,128,128]{3,2,1,0:T(8,128)}, u32[]{:S(2)}, u32[]{:S(2)}) collective-permute-start(f32[1,8,128,128]{3,2,1,0:T(8,128)} %fusion.81), channel_id=1, source_target_pairs={{0,16},{2,18},{4,20},{6,22},{8,24},{10,26},{12,28},{14,30},{16,0},... | collective-permute-start | bytes 1572872 | tf_op jit(solution)/shard_map/ppermute | solution.py:10
  649.6 12.9 %copy-start.4 = (bf16[2048,8,128]{0,2,1:T(8,128)(2,1)S(1)}, bf16[2048,8,128]{0,2,1:T(8,128)(2,1)}, u32[]{:S(2)}) copy-start(bf16[2048,8,128]{0,2,1:T(8,128)(2,1)} %get-tuple-element.334) | copy-start | bytes 12582916
  660.7 2.2 copy-start.2
  680.7 1.6 copy-start.7
  680.7 8.6 %copy-start.9 = (f32[2048,8]{0,1:T(8,128)S(1)}, f32[2048,8]{0,1:T(8,128)}, u32[]{:S(2)}) copy-start(f32[2048,8]{0,1:T(8,128)} %copy-done.8) | copy-start | bytes 196612
  680.7 8.6 %copy-start.11 = (f32[2048,8]{0,1:T(8,128)S(1)}, f32[2048,8]{0,1:T(8,128)}, u32[]{:S(2)}) copy-start(f32[2048,8]{0,1:T(8,128)} %copy-done.10) | copy-start | bytes 196612
  680.7 8.6 %copy-start.13 = (f32[2048,8]{0,1:T(8,128)S(1)}, f32[2048,8]{0,1:T(8,128)}, u32[]{:S(2)}) copy-start(f32[2048,8]{0,1:T(8,128)} %copy-done.12) | copy-start | bytes 196612
  680.7 8.6 %copy-start.15 = (f32[2048,8]{0,1:T(8,128)S(1)}, f32[2048,8]{0,1:T(8,128)}, u32[]{:S(2)}) copy-start(f32[2048,8]{0,1:T(8,128)} %copy-done.14) | copy-start | bytes 196612
Sparse Core Ops, SparseCore 0:
  96.3 91.4 all-gather.2
where the time goes:
time: 736 us; the launch traced here: 722 us
  matrix products  391 us (53%)
  local copies, waits for them, and re-layouts  241 us (33%)
  waiting for transfers between devices  38.5 us (5%)
  between operations  14.6 us (2%)
  loops' own time  11.8 us (2%)
  other arithmetic  11.2 us (2%)
  starting transfers between devices  7.88 us (1%)
    dynamic_update_slice x4, local copies, waits for them, and re-layouts, group_terms(): lax.scan(one_block, (zero_grads, zero_grads), block_ids)  166 us
    dot_general x2, matrix products, one_block(): jnp.einsum('qhd,khd->hqk', query_blk, key_heads, preferred_element_type=j...  90.7 us
    unnamed x42, local copies, waits for them, and re-layouts  60.4 us
    dot_general x2, matrix products, one_block(): jnp.einsum('hqk,qhd->khd', prod_weighted, query_blk, preferred_element_ty...  57.5 us
    dot_general x2, matrix products, one_block(): jnp.einsum('hqk,qhd->khd', score_weighted, cotan_blk, preferred_element_t...  57.3 us
    dot_general x2, matrix products, one_block(): jnp.einsum('hqk,khd->qhd', prod_weighted, key_heads, preferred_element_ty...  53.5 us
    dot_general x2, matrix products, one_block(): jnp.einsum('qhd,khd->hqk', cotan_blk, value_heads, preferred_element_type...  52.5 us
    ppermute x4, waiting for transfers between devices, partner(): lax.ppermute(shard, axis, [(i, i ^ 1 << distance) for i in range(lax.axis...  38.5 us
  transfers between devices with their start and end apart: 5, of which 2 were waited for; matrix products, arithmetic and copies ran while one was open for 77% of the time, Pallas kernels for 0%

commit v1 on v0

v1 whole, which is shorter than its diff:
```python
import functools

import jax
import jax.numpy as jnp
from jax import lax
from jax.experimental import pallas as pl
from jax.experimental.pallas import tpu as pltpu
from jax.sharding import PartitionSpec as P

F32 = jnp.float32
BF16 = jnp.bfloat16
VMEM_LIMIT = 56 * 1024 * 1024


def dot(lhs, rhs, contract=((1,), (0,))):
    return lax.dot_general(lhs, rhs, (contract, ((), ())), preferred_element_type=F32)


def softplus(x):
    return jnp.maximum(x, 0.0) + jnp.log1p(jnp.exp(-jnp.abs(x)))


def states_kernel(scaling, chunk, q_ref, k_ref, v_ref, d_ref, logit_ref, sloc_ref, dloc_ref, g_ref, ds_ref):
    rows, dk = q_ref.shape
    levels = logit_ref.shape[1]
    weights = scaling * softplus(logit_ref[0])
    state = jnp.zeros((dk, dk), F32)
    outer = jnp.zeros(((levels - 1) * dk, dk), F32)
    own = []
    for j in range(rows // chunk):
        part = slice(j * chunk, (j + 1) * chunk)
        k_t = k_ref[part, :].T
        q_t = q_ref[part, :].T.astype(F32)
        sloc_ref[0, j] = state.astype(BF16)
        state = state + dot(k_t, v_ref[part, :])
        weighted = jnp.concatenate(
            [(weights[l : l + 1, part] * q_t).astype(BF16) for l in range(levels)], axis=0
        )
        adjoint = dot(weighted, d_ref[part, :])
        own.append(adjoint[:dk])
        outer = outer + adjoint[dk:]
    g_ref[0] = state
    for l in range(levels - 1):
        ds_ref[l, 0] = outer[l * dk : (l + 1) * dk]
    after = jnp.zeros((dk, dk), F32)
    for j in reversed(range(rows // chunk)):
        dloc_ref[0, j] = after.astype(BF16)
        after = after + own[j]


def grads_kernel(
    scaling, chunk, q_ref, k_ref, v_ref, d_ref, logit_ref, sloc_ref, dloc_ref, s_ref, dg_ref,
    gq_ref, gk_ref, gv_ref, lg_ref, cot_ref,
):
    rows, dk = q_ref.shape
    levels = logit_ref.shape[1]
    logits = logit_ref[0]
    gates = softplus(logits)
    weights = scaling * gates
    gate_slope = jax.nn.sigmoid(logits)
    slope = [gate_slope[l : l + 1] * (scaling if l else 1.0 / gates[0:1]) for l in range(levels)]
    outer_states = jnp.concatenate([s_ref[l, 0] for l in range(levels - 1)], axis=0)
    causal = lax.broadcasted_iota(jnp.int32, (chunk, chunk), 0) <= lax.broadcasted_iota(
        jnp.int32, (chunk, chunk), 1
    )
    for j in range(rows // chunk):
        part = slice(j * chunk, (j + 1) * chunk)
        q, k, v, d = q_ref[part, :], k_ref[part, :], v_ref[part, :], d_ref[part, :]
        q_t, k_t, d_t = q.T, k.T, d.T
        w0 = weights[0:1, part]
        spread = jnp.where(causal, w0, 0.0)
        score_w = (spread * dot(k, q_t)).astype(BF16)
        prod_w = (spread * dot(v, d_t)).astype(BF16)
        q_f = q_t.astype(F32)
        total = dot(k_t, prod_w) + w0 * dot(sloc_ref[0, j], d_t)
        terms = [jnp.sum(q_f * total, axis=0, keepdims=True) * slope[0][:, part]]
        mapped = dot(outer_states, d_t)
        for l in range(1, levels):
            own = mapped[(l - 1) * dk : l * dk]
            total = total + weights[l : l + 1, part] * own
            terms.append(jnp.sum(q_f * own, axis=0, keepdims=True) * slope[l][:, part])
        level_grad = jnp.concatenate(terms, axis=0)
        lg_ref[0, :, part] = level_grad
        cot_ref[0, :, part] = level_grad.astype(BF16)
        gq_ref[part, :] = total.astype(BF16).T
        carried = (dloc_ref[0, j].astype(F32) + dg_ref[0]).astype(BF16)
        gk_ref[part, :] = (dot(prod_w, q) + dot(v, carried, ((1,), (1,)))).astype(BF16)
        gv_ref[part, :] = (dot(score_w, d) + dot(k, carried)).astype(BF16)


def exchange_kernel(bits, g_ref, ds_ref, s_ref, dg_ref, *scratch):
    (g_out, g_in, f_out, f_in, c_in, d_out, d_in, d0_out, d0_in, a_out, a_in, t_out, t_in, send_sem, recv_sem) = scratch
    me = lax.axis_index("ctx")
    heads = g_ref.shape[0]
    half = heads // 2
    core = me % 2
    mine, other = pl.ds(core * half, half), pl.ds((1 - core) * half, half)
    peers = [me + (1 << b) - 2 * (1 << b) * ((me // (1 << b)) % 2) for b in range(bits)]
    upper = [((me // (1 << b)) % 2).astype(F32) for b in range(bits)]

    barrier = pltpu.get_barrier_semaphore()
    for peer in peers:
        pl.semaphore_signal(barrier, inc=1, device_id={"ctx": peer}, device_id_type=pl.DeviceIdType.MESH)

    for b in range(1, bits):
        d_out[b - 1] = (upper[b] * ds_ref[b, other]).astype(BF16)
    g_out[...] = g_ref[...].astype(BF16)
    d0_out[...] = (upper[0] * ds_ref[0]).astype(BF16)
    pl.semaphore_wait(barrier, bits)

    copies = []

    def send(src, dst, b):
        i = len(copies)
        copy = pltpu.make_async_remote_copy(
            src_ref=src, dst_ref=dst, send_sem=send_sem.at[i], recv_sem=recv_sem.at[i],
            device_id={"ctx": peers[b]}, device_id_type=pl.DeviceIdType.MESH,
        )
        copy.start()
        copies.append(copy)
        return copy

    d_copy = send(d_out, d_in, 0)
    g_copy = send(g_out, g_in, 0)
    d0_copy = send(d0_out, d0_in, 0)

    carried = jnp.zeros((half,) + g_ref.shape[1:], F32)

    def send_adjoint(b, carried):
        pair = upper[b] * ds_ref[b, mine] + d_in[b - 1].astype(F32)
        a_out[b - 1] = (carried + pair).astype(BF16)
        return send(a_out.at[b - 1], a_in.at[b - 1], b)

    d_copy.wait_recv()
    a_copy = send_adjoint(bits - 1, carried)
    g_copy.wait_recv()
    block = g_ref[mine] + g_in[mine].astype(F32)
    f_out[0] = block.astype(BF16)
    f_copy = send(f_out.at[0], f_in.at[0], 1)
    s_ref[0] = g_in[...] * upper[0].astype(BF16)

    forwards = []

    def forward_step(b, block, f_copy):
        f_copy.wait_recv()
        if b + 1 < bits:
            block = block + f_in[b - 1].astype(F32)
            f_out[b] = block.astype(BF16)
            f_copy = send(f_out.at[b], f_in.at[b], b + 1)
        forwards.append(send(f_in.at[b - 1], c_in.at[b - 1], 0))
        s_ref[b, mine] = f_in[b - 1] * upper[b].astype(BF16)
        return block, f_copy

    def adjoint_step(b, carried, a_copy):
        a_copy.wait_recv()
        carried = carried + a_in[b - 1].astype(F32)
        if b > 1:
            return carried, send_adjoint(b - 1, carried)
        t_out[...] = carried.astype(BF16)
        return carried, send(t_out, t_in, 0)

    for b in range(1, bits):
        if b + 1 < bits:
            block, f_copy = forward_step(b, block, f_copy)
        carried, a_copy = adjoint_step(bits - b, carried, a_copy)
        if b + 1 == bits:
            block, f_copy = forward_step(b, block, f_copy)
    d0_copy.wait_recv()
    dg_ref[mine] = carried + d0_in[mine].astype(F32)
    a_copy.wait_recv()
    dg_ref[other] = t_in[...].astype(F32) + d0_in[other].astype(F32)
    for b in range(1, bits):
        forwards[b - 1].wait_recv()
        s_ref[b, other] = c_in[b - 1] * upper[b].astype(BF16)
    for copy in copies:
        copy.wait_send()


def exchange(state, adjoints):
    heads, dk, _ = state.shape
    bits = adjoints.shape[0]
    half = heads // 2
    whole, parts, one = (heads, dk, dk), (bits - 1, half, dk, dk), (half, dk, dk)
    shapes = [whole, whole, parts, parts, parts, parts, parts, whole, whole, parts, parts, one, one]
    count = 4 + 3 * (bits - 1)
    return pl.pallas_call(
        functools.partial(exchange_kernel, bits),
        in_specs=[pl.BlockSpec(memory_space=pltpu.VMEM)] * 2,
        out_specs=[pl.BlockSpec(memory_space=pltpu.VMEM)] * 2,
        out_shape=[
            jax.ShapeDtypeStruct((bits, heads, dk, dk), BF16),
            jax.ShapeDtypeStruct((heads, dk, dk), F32),
        ],
        scratch_shapes=[pltpu.VMEM(s, BF16) for s in shapes]
        + [pltpu.SemaphoreType.DMA((count,)), pltpu.SemaphoreType.DMA((count,))],
        compiler_params=pltpu.CompilerParams(
            collective_id=0, has_side_effects=True, vmem_limit_bytes=VMEM_LIMIT
        ),
        name="exchange",
    )(state, adjoints)


def body(queries, key_vectors, values, out_grad, level_logits, level_proj):
    rows, width = queries.shape
    heads, levels, _ = level_logits.shape
    dk = width // heads
    scaling = float(dk * rows * lax.axis_size("ctx")) ** (-0.5)
    chunk = min(256, rows)
    chunks = rows // chunk
    big = pl.BlockSpec((rows, dk), lambda h: (0, h))
    gate = pl.BlockSpec((1, levels, rows), lambda h: (h, 0, 0))
    local = pl.BlockSpec((1, chunks, dk, dk), lambda h: (h, 0, 0, 0))
    single = pl.BlockSpec((1, dk, dk), lambda h: (h, 0, 0))
    stacked = pl.BlockSpec((levels - 1, 1, dk, dk), lambda h: (0, h, 0, 0))
    shape = jax.ShapeDtypeStruct
    params = pltpu.CompilerParams(vmem_limit_bytes=VMEM_LIMIT)
    before, after, state, adjoints = pl.pallas_call(
        functools.partial(states_kernel, scaling, chunk),
        grid=(heads,),
        in_specs=[big, big, big, big, gate],
        out_specs=[local, local, single, stacked],
        out_shape=[
            shape((heads, chunks, dk, dk), BF16),
            shape((heads, chunks, dk, dk), BF16),
            shape((heads, dk, dk), F32),
            shape((levels - 1, heads, dk, dk), F32),
        ],
        compiler_params=params,
        name="states",
    )(queries, key_vectors, values, out_grad, level_logits)
    level_states, carried = exchange(state, adjoints)
    grad_q, grad_k, grad_v, level_grad, logit_cot = pl.pallas_call(
        functools.partial(grads_kernel, scaling, chunk),
        grid=(heads,),
        in_specs=[big, big, big, big, gate, local, local, stacked, single],
        out_specs=[big, big, big, gate, gate],
        out_shape=[
            shape((rows, width), BF16),
            shape((rows, width), BF16),
            shape((rows, width), BF16),
            shape((heads, levels, rows), F32),
            shape((heads, levels, rows), BF16),
        ],
        compiler_params=params,
        name="grads",
    )(queries, key_vectors, values, out_grad, level_logits, before, after, level_states, carried)
    hidden_grad = lax.dot_general(
        lax.all_gather(logit_cot.reshape(-1, rows), "head", axis=0, tiled=True),
        level_proj,
        (((0,), (0,)), ((), ())),
        preferred_element_type=F32,
    )
    return grad_q, grad_k, grad_v, level_grad, hidden_grad.astype(BF16)


def solution(mesh):
    in_specs = (
        P("ctx", "head"),
        P("ctx", "head"),
        P("ctx", "head"),
        P("ctx", "head"),
        P("head", None, "ctx"),
        P(None, "head"),
    )
    out_specs = (
        P("ctx", "head"),
        P("ctx", "head"),
        P("ctx", "head"),
        P("head", None, "ctx"),
        P("ctx", "head"),
    )
    return jax.shard_map(body, mesh=mesh, in_specs=in_specs, out_specs=out_specs, check_vma=False)
```

time: 736 us -> 85.3 us (0.12); the launches traced: 722 us -> 84.9 us
  matrix products: 391 us -> 3.29 us
  local copies, waits for them, and re-layouts: 241 us -> 5 us
  Pallas kernels: 0 us -> 68.7 us
  waiting for transfers between devices: 38.5 us -> 0 us
  between operations: 14.6 us -> 0.66 us
  loops' own time: 11.8 us -> 0 us
  other arithmetic: 11.2 us -> 0 us
  starting transfers between devices: 7.88 us -> 0 us
    dot_general x27 -> x1, matrix products: 391 us -> 3.29 us  [body(): lax.dot_general(lax.all_gather(logit_cot.reshape(-1, rows), 'head', axis=...]
    dynamic_update_slice x4 -> x0, local copies, waits for them, and re-layouts: 166 us -> none  [group_terms(): lax.scan(one_block, (zero_grads, zero_grads), block_ids)]
    pallas_call x0 -> x3, Pallas kernels: none -> 68.7 us  [the longest x1 30.9 us: exchange(): pl.pallas_call(functools.partial(exchange_kernel, bits), in_specs=[pl.Blo...]
    unnamed x42 -> x4, local copies, waits for them, and re-layouts: 60.4 us -> 3.97 us
    ppermute x4 -> x0, waiting for transfers between devices: 38.5 us -> none  [partner(): lax.ppermute(shard, axis, [(i, i ^ 1 << distance) for i in range(lax.axis...]
    another operation x1 -> x0, loops' own time: 11.8 us -> none  [group_terms(): lax.scan(one_block, (zero_grads, zero_grads), block_ids)]
    reshape x2 -> x1, local copies, waits for them, and re-layouts: 11.9 us -> 1.03 us  [body(): logit_cot.reshape(-1, rows)]
    ppermute x4 -> x0, starting transfers between devices: 7.85 us -> none  [partner(): lax.ppermute(shard, axis, [(i, i ^ 1 << distance) for i in range(lax.axis...]
  transfers between devices with their start and end apart: 5 -> 0, of which waited for: 2 -> 0; matrix products, arithmetic and copies ran while one was open for 77% -> 0% of each run, Pallas kernels for 0% -> 0%
where the time goes in v1:
time: 85.3 us; the launch traced here: 84.9 us
  Pallas kernels  68.7 us (81%)
  blocking collectives  7.22 us (8%)
  local copies, waits for them, and re-layouts  5 us (6%)
  matrix products  3.29 us (4%)
    pallas_call x1, Pallas kernels, exchange(): pl.pallas_call(functools.partial(exchange_kernel, bits), in_specs=[pl.Blo...  30.9 us
    pallas_call x1, Pallas kernels, body(): pl.pallas_call(functools.partial(grads_kernel, scaling, chunk), grid=(hea...  24.6 us
    pallas_call x1, Pallas kernels, body(): pl.pallas_call(functools.partial(states_kernel, scaling, chunk), grid=(he...  13.1 us
    all_gather x1, blocking collectives, body(): lax.all_gather(logit_cot.reshape(-1, rows), 'head', axis=0, tiled=True)  7.22 us
    unnamed x4, local copies, waits for them, and re-layouts  3.97 us
    dot_general x1, matrix products, body(): lax.dot_general(lax.all_gather(logit_cot.reshape(-1, rows), 'head', axis=...  3.29 us

profile of v1, /device:TPU:0, one launch (start us, length us, event | category | flops | bytes accessed | tf_op | source)
XLA Modules:
  0.0 84.9 jit_solution(15773203838116843374)
XLA Ops:
  0.6 0.0 copy-start
  0.6 2.0 %copy.15.logit_ref = f32[8,5,2048]{2,1,0:T(8,128)} copy(f32[8,5,2048]{2,0,1:T(8,128)} %param.10) | data formatting | bytes 655360 | tf_op args[4]
  2.6 13.1 %states.1 = (bf16[8,8,128,128]{3,2,1,0:T(8,128)(2,1)}, bf16[8,8,128,128]{3,2,1,0:T(8,128)(2,1)}, f32[8,128,128]{2,1,0:T(8,128)}, f32[4,8,128,128]{3,2,1,0:T(8,128)}) custom-call(bf16[2048,1024]{1,0:T(8,128)(2,1)} %q_ref.3, bf16[2048,1024]{1,0:T(8,128)(2,1)} %k_ref.3, bf16[2048,1024]{1,0:T(8,128)(2,1)} %v_ref.3, bf16[2048,1024]{1,0:T(8,128)(2,1)} %d_ref.3, ...), custom_call_target="tpu_custom_call" | custom-call | tf_op jit(solution)/shard_map/states/pallas_call | solution.py:217
  15.8 30.9 %exchange.1 = (bf16[4,8,128,128]{3,2,1,0:T(8,128)(2,1)}, f32[8,128,128]{2,1,0:T(8,128)}) custom-call(f32[8,128,128]{2,1,0:T(8,128)} %get-tuple-element.18.g_ref, f32[4,8,128,128]{3,2,1,0:T(8,128)} %get-tuple-element.19.ds_ref), custom_call_target="tpu_custom_call" | custom-call | tf_op jit(solution)/shard_map/exchange/pallas_call | solution.py:186
  46.7 24.6 %grads.1 = (bf16[2048,1024]{1,0:T(8,128)(2,1)}, bf16[2048,1024]{1,0:T(8,128)(2,1)}, bf16[2048,1024]{1,0:T(8,128)(2,1)}, f32[8,5,2048]{2,1,0:T(8,128)}, bf16[8,5,2048]{2,1,0:T(8,128)(2,1)}) custom-call(bf16[2048,1024]{1,0:T(8,128)(2,1)} %q_ref.3, bf16[2048,1024]{1,0:T(8,128)(2,1)} %k_ref.3, bf16[2048,1024]{1,0:T(8,128)(2,1)} %v_ref.3, ...), custom_call_target="tpu_custom_call" | custom-call | tf_op jit(solution)/shard_map/grads/pallas_call | solution.py:232
  71.4 1.0 %reshape.13 = bf16[40,2048]{1,0:T(8,128)(2,1)S(1)} reshape(bf16[8,5,2048]{2,1,0:T(8,128)(2,1)} %get-tuple-element.26) | data formatting | bytes 327680 | tf_op jit(solution)/shard_map/reshape | solution.py:248
  72.4 7.2 %all_gather.3 = bf16[80,2048]{1,0:T(8,128)(2,1)S(1)} all-gather(bf16[40,2048]{1,0:T(8,128)(2,1)S(1)} %reshape.13), channel_id=1, replica_groups=mesh['ctx'=16,'head'=2] {'head'}, dimensions={0}, use_global_device_ids=true | all-gather | bytes 491520 | tf_op jit(solution)/shard_map/all_gather | solution.py:248
  79.6 2.0 %copy.16 = f32[8,5,2048]{2,0,1:T(8,128)} copy(f32[8,5,2048]{2,1,0:T(8,128)} %get-tuple-element.35) | data formatting | bytes 655360
  81.6 0.0 copy-done
  81.6 3.3 %convolution_convert_fusion = bf16[2048,1024]{1,0:T(8,128)(2,1)} fusion(bf16[80,2048]{1,0:T(8,128)(2,1)S(1)} %all_gather.3, bf16[80,1024]{1,0:T(8,128)(2,1)S(1)} %copy-done), kind=kOutput, calls=%fused_computation | convolution fusion | flops 337641472 | bytes 4685824 | tf_op jit(solution)/shard_map/dot_general | solution.py:247
Async XLA Ops:
  0.6 80.9 %copy-start = (bf16[80,1024]{1,0:T(8,128)(2,1)S(1)}, bf16[80,1024]{1,0:T(8,128)(2,1)}, u32[]{:S(2)}) copy-start(bf16[80,1024]{1,0:T(8,128)(2,1)} %param.11) | copy-start | bytes 491524

commit v2 on v1

--- a/solution.py
+++ b/solution.py
@@ -48,9 +48,14 @@
         after = after + own[j]
 
 
-def grads_kernel(
-    scaling, chunk, q_ref, k_ref, v_ref, d_ref, logit_ref, sloc_ref, dloc_ref, s_ref, dg_ref,
-    gq_ref, gk_ref, gv_ref, lg_ref, cot_ref,
+def causal_mask(chunk):
+    return lax.broadcasted_iota(jnp.int32, (chunk, chunk), 0) <= lax.broadcasted_iota(
+        jnp.int32, (chunk, chunk), 1
+    )
+
+
+def query_kernel(
+    scaling, chunk, q_ref, k_ref, v_ref, d_ref, logit_ref, sloc_ref, s_ref, gq_ref, lg_ref, cot_ref
 ):
     rows, dk = q_ref.shape
     levels = logit_ref.shape[1]
@@ -60,17 +65,12 @@
     gate_slope = jax.nn.sigmoid(logits)
     slope = [gate_slope[l : l + 1] * (scaling if l else 1.0 / gates[0:1]) for l in range(levels)]
     outer_states = jnp.concatenate([s_ref[l, 0] for l in range(levels - 1)], axis=0)
-    causal = lax.broadcasted_iota(jnp.int32, (chunk, chunk), 0) <= lax.broadcasted_iota(
-        jnp.int32, (chunk, chunk), 1
-    )
+    causal = causal_mask(chunk)
     for j in range(rows // chunk):
         part = slice(j * chunk, (j + 1) * chunk)
-        q, k, v, d = q_ref[part, :], k_ref[part, :], v_ref[part, :], d_ref[part, :]
-        q_t, k_t, d_t = q.T, k.T, d.T
+        q_t, k_t, d_t = q_ref[part, :].T, k_ref[part, :].T, d_ref[part, :].T
         w0 = weights[0:1, part]
-        spread = jnp.where(causal, w0, 0.0)
-        score_w = (spread * dot(k, q_t)).astype(BF16)
-        prod_w = (spread * dot(v, d_t)).astype(BF16)
+        prod_w = (jnp.where(causal, w0, 0.0) * dot(v_ref[part, :], d_t)).astype(BF16)
         q_f = q_t.astype(F32)
         total = dot(k_t, prod_w) + w0 * dot(sloc_ref[0, j], d_t)
         terms = [jnp.sum(q_f * total, axis=0, keepdims=True) * slope[0][:, part]]
@@ -83,6 +83,20 @@
         lg_ref[0, :, part] = level_grad
         cot_ref[0, :, part] = level_grad.astype(BF16)
         gq_ref[part, :] = total.astype(BF16).T
+
+
+def key_value_kernel(
+    scaling, chunk, q_ref, k_ref, v_ref, d_ref, logit_ref, dloc_ref, dg_ref, gk_ref, gv_ref
+):
+    rows, dk = q_ref.shape
+    weights = scaling * softplus(logit_ref[0])
+    causal = causal_mask(chunk)
+    for j in range(rows // chunk):
+        part = slice(j * chunk, (j + 1) * chunk)
+        q, k, v, d = q_ref[part, :], k_ref[part, :], v_ref[part, :], d_ref[part, :]
+        spread = jnp.where(causal, weights[0:1, part], 0.0)
+        score_w = (spread * dot(k, q.T)).astype(BF16)
+        prod_w = (spread * dot(v, d.T)).astype(BF16)
         carried = (dloc_ref[0, j].astype(F32) + dg_ref[0]).astype(BF16)
         gk_ref[part, :] = (dot(prod_w, q) + dot(v, carried, ((1,), (1,)))).astype(BF16)
         gv_ref[part, :] = (dot(score_w, d) + dot(k, carried)).astype(BF16)
@@ -229,26 +243,40 @@
         name="states",
     )(queries, key_vectors, values, out_grad, level_logits)
     level_states, carried = exchange(state, adjoints)
-    grad_q, grad_k, grad_v, level_grad, logit_cot = pl.pallas_call(
-        functools.partial(grads_kernel, scaling, chunk),
+    wide = shape((rows, width), BF16)
+    grad_q, level_grad, logit_cot = pl.pallas_call(
+        functools.partial(query_kernel, scaling, chunk),
         grid=(heads,),
-        in_specs=[big, big, big, big, gate, local, local, stacked, single],
-        out_specs=[big, big, big, gate, gate],
-        out_shape=[
-            shape((rows, width), BF16),
-            shape((rows, width), BF16),
-            shape((rows, width), BF16),
-            shape((heads, levels, rows), F32),
-            shape((heads, levels, rows), BF16),
-        ],
+        in_specs=[big, big, big, big, gate, local, stacked],
+        out_specs=[big, gate, gate],
+        out_shape=[wide, shape((heads, levels, rows), F32), shape((heads, levels, rows), BF16)],
         compiler_params=params,
-        name="grads",
-    )(queries, key_vectors, values, out_grad, level_logits, before, after, level_states, carried)
+        name="query_grads",
+    )(queries, key_vectors, values, out_grad, level_logits, before, level_states)
+    own_cot = logit_cot.reshape(heads * levels, rows)
+    slices = lax.axis_size("head")
+    gathered = [own_cot] + [
+        lax.ppermute(own_cot, "head", [(i, (i - hop) % slices) for i in range(slices)])
+        for hop in range(1, slices)
+    ]
+    grad_k, grad_v = pl.pallas_call(
+        functools.partial(key_value_kernel, scaling, chunk),
+        grid=(heads,),
+        in_specs=[big, big, big, big, gate, local, single],
+        out_specs=[big, big],
+        out_shape=[wide, wide],
+        compiler_params=params,
+        cost_estimate=pl.CostEstimate(
+            flops=2 * rows * width * (4 * chunk + 2 * dk), bytes_accessed=12 * rows * width, transcendentals=0
+        ),
+        name="key_value_grads",
+    )(queries, key_vectors, values, out_grad, level_logits, after, carried)
+    turned = lax.dynamic_slice_in_dim(
+        jnp.concatenate([level_proj, level_proj], axis=0),
+        lax.axis_index("head") * heads * levels, level_proj.shape[0], 0,
+    )
     hidden_grad = lax.dot_general(
-        lax.all_gather(logit_cot.reshape(-1, rows), "head", axis=0, tiled=True),
-        level_proj,
-        (((0,), (0,)), ((), ())),
-        preferred_element_type=F32,
+        jnp.concatenate(gathered, axis=0), turned, (((0,), (0,)), ((), ())), preferred_element_type=F32
     )
     return grad_q, grad_k, grad_v, level_grad, hidden_grad.astype(BF16)
 

time: 85.3 us -> 91.4 us (1.072)
  Pallas kernels: 68.7 us -> 81.3 us
  blocking collectives: 7.22 us -> 0 us
  starting transfers between devices: 0 us -> 1.56 us
  local copies, waits for them, and re-layouts: 5 us -> 3.92 us
    pallas_call x1 -> x2, Pallas kernels: 24.6 us -> 37.2 us  [the longest x1 19.6 us: body(): pl.pallas_call(functools.partial(query_kernel, scaling, chunk), grid=(hea...]
    all_gather x1 -> x0, blocking collectives: 7.22 us -> none  [body(): lax.all_gather(logit_cot.reshape(-1, rows), 'head', axis=0, tiled=True)]
    ppermute x0 -> x1, starting transfers between devices: none -> 1.56 us  [body(): lax.ppermute(own_cot, 'head', [(i, (i - hop) % slices) for i in range(sli...]
    unnamed x4 -> x6, local copies, waits for them, and re-layouts: 3.97 us -> 2.89 us
  transfers between devices with their start and end apart: 0 -> 1, of which waited for: 0 -> 0; matrix products, arithmetic and copies ran while one was open for 0% -> 1% of each run, Pallas kernels for 0% -> 19%
where the time goes in v2:
time: 91.4 us; the launch traced here: 90.7 us
  Pallas kernels  81.3 us (89%)
  local copies, waits for them, and re-layouts  3.92 us (4%)
  matrix products  3.32 us (4%)
  starting transfers between devices  1.56 us (2%)
    pallas_call x1, Pallas kernels, exchange(): pl.pallas_call(functools.partial(exchange_kernel, bits), in_specs=[pl.Blo...  30.9 us
    pallas_call x1, Pallas kernels, body(): pl.pallas_call(functools.partial(query_kernel, scaling, chunk), grid=(hea...  19.6 us
    pallas_call x1, Pallas kernels, body(): pl.pallas_call(functools.partial(key_value_kernel, scaling, chunk), grid=...  17.6 us
    pallas_call x1, Pallas kernels, body(): pl.pallas_call(functools.partial(states_kernel, scaling, chunk), grid=(he...  13.1 us
    dot_general x1, matrix products, body(): lax.dot_general(jnp.concatenate(gathered, axis=0), turned, (((0,), (0,)),...  3.32 us
    unnamed x6, local copies, waits for them, and re-layouts  2.89 us
  transfers between devices with their start and end apart: 1, of which 0 were waited for; matrix products, arithmetic and copies ran while one was open for 1% of the time, Pallas kernels for 19%

profile of v2, /device:TPU:0, one launch (start us, length us, event | category | flops | bytes accessed | tf_op | source)
XLA Modules:
  0.0 90.7 jit_solution(8213945300230212901)
XLA Ops:
  0.6 2.0 %copy.16.logit_ref = f32[8,5,2048]{2,1,0:T(8,128)} copy(f32[8,5,2048]{2,0,1:T(8,128)} %param.10) | data formatting | bytes 655360 | tf_op args[4]
  2.6 13.1 %states.1 = (bf16[8,8,128,128]{3,2,1,0:T(8,128)(2,1)}, bf16[8,8,128,128]{3,2,1,0:T(8,128)(2,1)}, f32[8,128,128]{2,1,0:T(8,128)}, f32[4,8,128,128]{3,2,1,0:T(8,128)}) custom-call(bf16[2048,1024]{1,0:T(8,128)(2,1)} %q_ref.5, bf16[2048,1024]{1,0:T(8,128)(2,1)} %k_ref.5, bf16[2048,1024]{1,0:T(8,128)(2,1)} %v_ref.5, bf16[2048,1024]{1,0:T(8,128)(2,1)} %d_ref.5, ...), custom_call_target="tpu_custom_call" | custom-call | tf_op jit(solution)/shard_map/states/pallas_call | solution.py:231
  15.7 30.9 %exchange.1 = (bf16[4,8,128,128]{3,2,1,0:T(8,128)(2,1)}, f32[8,128,128]{2,1,0:T(8,128)}) custom-call(f32[8,128,128]{2,1,0:T(8,128)} %get-tuple-element.17.g_ref, f32[4,8,128,128]{3,2,1,0:T(8,128)} %get-tuple-element.18.ds_ref), custom_call_target="tpu_custom_call" | custom-call | tf_op jit(solution)/shard_map/exchange/pallas_call | solution.py:200
  46.7 19.6 %query_grads.1 = (bf16[2048,1024]{1,0:T(8,128)(2,1)}, f32[8,5,2048]{2,1,0:T(8,128)}, bf16[8,5,2048]{2,1,0:T(8,128)(2,1)}) custom-call(bf16[2048,1024]{1,0:T(8,128)(2,1)} %q_ref.5, bf16[2048,1024]{1,0:T(8,128)(2,1)} %k_ref.5, bf16[2048,1024]{1,0:T(8,128)(2,1)} %v_ref.5, bf16[2048,1024]{1,0:T(8,128)(2,1)} %d_ref.5, f32[8,5,2048]{2,1,0:T(8,128)} %copy.16.logit_ref, ...), custom_call_target="tpu_custom_call" | custom-call | tf_op jit(solution)/shard_map/query_grads/pallas_call | solution.py:247
  66.3 1.0 %reshape.13 = bf16[40,2048]{1,0:T(8,128)(2,1)S(1)} reshape(bf16[8,5,2048]{2,1,0:T(8,128)(2,1)} %get-tuple-element.26) | data formatting | bytes 327680 | tf_op jit(solution)/shard_map/reshape | solution.py:256
  67.3 1.6 %collective-permute-start = (bf16[40,2048]{1,0:T(8,128)(2,1)S(1)}, bf16[40,2048]{1,0:T(8,128)(2,1)S(1)}, u32[]{:S(2)}, u32[]{:S(2)}) collective-permute-start(bf16[40,2048]{1,0:T(8,128)(2,1)S(1)} %reshape.13), channel_id=1, source_target_pairs={{0,1},{1,0},{2,3},{3,2},{4,5},{5,4},{6,7},{7,6},{8,9},{9,8},{10,11... | collective-permute-start | bytes 491528 | tf_op jit(solution)/shard_map/ppermute | solution.py:259
  68.9 0.0 copy-start
  68.9 0.0 copy-start.1
  68.9 17.6 %key_value_grads.1 = (bf16[2048,1024]{1,0:T(8,128)(2,1)}, bf16[2048,1024]{1,0:T(8,128)(2,1)}) custom-call(bf16[2048,1024]{1,0:T(8,128)(2,1)} %q_ref.5, bf16[2048,1024]{1,0:T(8,128)(2,1)} %k_ref.5, bf16[2048,1024]{1,0:T(8,128)(2,1)} %v_ref.5, bf16[2048,1024]{1,0:T(8,128)(2,1)} %d_ref.5, f32[8,5,2048]{2,1,0:T(8,128)} %copy.16.logit_ref, ...), custom_call_target="tpu_custom_call" | custom-call | flops 5368709120 | bytes 25165824 | tf_op jit(solution)/shard_map/key_value_grads/pallas_call | solution.py:262
  86.5 0.0 copy-done
  86.5 0.9 %copy.18 = f32[8,5,2048]{2,0,1:T(8,128)} copy(f32[8,5,2048]{2,1,0:T(8,128)S(1)} %copy-done) | data formatting | bytes 655360
  87.4 0.0 collective-permute-done
  87.4 0.0 copy-done.1
  87.4 3.3 %convolution_convert_fusion = bf16[2048,1024]{1,0:T(8,128)(2,1)} fusion(bf16[40,2048]{1,0:T(8,128)(2,1)S(1)} %collective-permute-done, bf16[40,2048]{1,0:T(8,128)(2,1)S(1)} %reshape.13, s32[]{:T(128)S(6)} %select_n.3, bf16[80,1024]{1,0:T(8,128)(2,1)S(1)} %copy-done.1), kind=kOutput, calls=%fused_computation | convolution fusion | flops 338624512 | bytes 4685828 | tf_op jit(solution)/shard_map/dot_general | solution.py:278
Async XLA Ops:
  67.3 20.1 %collective-permute-start = (bf16[40,2048]{1,0:T(8,128)(2,1)S(1)}, bf16[40,2048]{1,0:T(8,128)(2,1)S(1)}, u32[]{:S(2)}, u32[]{:S(2)}) collective-permute-start(bf16[40,2048]{1,0:T(8,128)(2,1)S(1)} %reshape.13), channel_id=1, source_target_pairs={{0,1},{1,0},{2,3},{3,2},{4,5},{5,4},{6,7},{7,6},{8,9},{9,8},{10,11... | collective-permute-start | bytes 491528 | tf_op jit(solution)/shard_map/ppermute | solution.py:259
  68.9 17.6 %copy-start = (f32[8,5,2048]{2,1,0:T(8,128)S(1)}, f32[8,5,2048]{2,1,0:T(8,128)}, u32[]{:S(2)}) copy-start(f32[8,5,2048]{2,1,0:T(8,128)} %get-tuple-element.35) | copy-start | bytes 983044
  68.9 18.5 %copy-start.1 = (bf16[80,1024]{1,0:T(8,128)(2,1)S(1)}, bf16[80,1024]{1,0:T(8,128)(2,1)}, u32[]{:S(2)}) copy-start(bf16[80,1024]{1,0:T(8,128)(2,1)} %param.11) | copy-start | bytes 491524
